TPU v7x, 32 devices: a whole 2x2x4 slice. The times are simulated.
32 devices in a mesh: dp: 8 (over z, core), mp: 4 (over y, x).
Axes of the slice: x: 2, y: 2, z: 4, core: 2. Of those that a mesh axis runs over, the one named last changes fastest.
Arguments:
- frames: bfloat16 [1536, 1536], P('dp', 'mp'), may hold values from -6 to 6
- frame_owner: int32 [1536, 1], P('dp'), may hold values from 0 to 7; in each aligned block of 192 rows (0 to 191, 192 to 383, ...) at most 32 rows name the same one
- frame_valid: int32 [1536], P('dp'), may hold values 0 or 1
- norm_gain: float32 [1536], replicated, may hold values from 0.1 to 1.9
- value_weight: bfloat16 [1536, 1536], P('dp', 'mp'), may hold values from -0.15625 to 0.15625
- gate_weight: bfloat16 [1536, 1536], P('dp', 'mp'), may hold values from -0.15625 to 0.15625
- grad_owned: bfloat16 [8, 8, 32, 1536], P('dp', None, None, 'mp'), may hold values from -6 to 6
Outputs:
- gated_owned: bfloat16 [8, 8, 32, 1536], P('dp', None, None, 'mp')
- value_grad: float32 [1536, 1536], P('dp', 'mp')
- gate_grad: float32 [1536, 1536], P('dp', 'mp')
- normed_grad: bfloat16 [8, 8, 32, 1536], P('dp', None, None, 'mp')
Inputs may be any that keep to these rules, and one draw needn't show every extreme that they name: `frame_owner`: within the rows of one device (aligned blocks of 192 rows) no owner is named more than 32 times, a bound that some block reaches.
All inputs are finite; a program needn't handle non-finite values. No bound on the sum of `frame_valid` on one device may be relied on, other than what follows from the above.
Results may differ from a plain program's by a relative error of at most 0.013.
Values may be sent and summed in bfloat16 or wider, within the bound.
A program may use at most 64 MiB of HBM per device.

v0:
```python
import jax
import jax.numpy as jnp
from jax import lax
from jax.sharding import PartitionSpec as P

epsilon = 1e-05


def normalize_project(whole, slot_live, norm_gain, value_full, gate_full):
    wide = whole.astype(jnp.float32)
    row_mean = jnp.mean(wide, axis=-1, keepdims=True)
    centred = wide - row_mean
    row_var = jnp.mean(centred * centred, axis=-1, keepdims=True)
    normed = (
        centred
        * lax.rsqrt(row_var + epsilon)
        * norm_gain
        * slot_live.astype(jnp.float32)[..., None]
    ).astype(jnp.bfloat16)
    value_act = jnp.einsum("skd,de->ske", normed, value_full, preferred_element_type=jnp.float32)
    gate_act = jnp.einsum("skd,de->ske", normed, gate_full, preferred_element_type=jnp.float32)
    return (normed, value_act, gate_act)


def column_term(normed_flat, delta):
    return lax.dot_general(
        normed_flat, delta, (((0,), (0,)), ((), ())), preferred_element_type=jnp.float32
    )


def body(frames, frame_owner, frame_valid, norm_gain, value_weight, gate_weight, grad_owned):
    peers = lax.axis_size("dp")
    capacity = grad_owned.shape[2]
    row_total = frames.shape[0]
    slot_total = peers * capacity
    dest_owner = frame_owner[:, 0]
    positions = jnp.arange(row_total, dtype=jnp.int32)
    earlier = positions[None, :] < positions[:, None]
    same_owner = dest_owner[:, None] == dest_owner[None, :]
    slot_index = jnp.sum((same_owner & earlier).astype(jnp.int32), axis=1)
    targets = dest_owner * capacity + slot_index
    placing = (jnp.arange(slot_total, dtype=jnp.int32)[:, None] == targets[None, :]).astype(
        jnp.bfloat16
    )
    send_buffer = (
        jnp.dot(placing, frames, preferred_element_type=jnp.float32)
        .astype(jnp.bfloat16)
        .reshape(peers, capacity, -1)
    )
    send_live = (
        jnp.dot(placing, frame_valid.astype(jnp.bfloat16), preferred_element_type=jnp.float32)
        .astype(jnp.bfloat16)
        .reshape(peers, capacity)
    )
    value_full, gate_full = (
        lax.all_gather(value_weight, "dp", axis=0, tiled=True),
        lax.all_gather(gate_weight, "dp", axis=0, tiled=True),
    )
    received_rows, live_recv = (
        lax.all_to_all(send_buffer, "dp", split_axis=0, concat_axis=0, tiled=True),
        lax.all_to_all(send_live, "dp", split_axis=0, concat_axis=0, tiled=True),
    )
    whole = lax.all_gather(received_rows, "mp", axis=2, tiled=True)
    normed, value_act, gate_act = normalize_project(
        whole, live_recv, norm_gain, value_full, gate_full
    )
    normed_flat = normed.reshape(slot_total, -1)
    value_flat = value_act.reshape(slot_total, -1)
    gate_sig = jax.nn.sigmoid(gate_act.reshape(slot_total, -1))
    live_col = live_recv.astype(jnp.float32).reshape(slot_total, 1)
    gated = (value_flat * gate_sig).astype(jnp.bfloat16)
    upstream = grad_owned.reshape(slot_total, -1).astype(jnp.float32)
    value_delta = (upstream * gate_sig * live_col).astype(jnp.bfloat16)
    gate_delta = (upstream * value_flat * gate_sig * (1.0 - gate_sig) * live_col).astype(
        jnp.bfloat16
    )
    scale = float(row_total * peers) ** (-0.5)
    both_delta = jnp.concatenate([value_delta, gate_delta], axis=1)
    both_grad = lax.psum_scatter(
        column_term(normed_flat, both_delta), "dp", scatter_dimension=0, tiled=True
    )
    split_width = value_delta.shape[1]
    value_grad = both_grad[:, :split_width] * scale
    gate_grad = both_grad[:, split_width:] * scale
    contract_last = (((1,), (1,)), ((), ()))
    partial_grad = lax.dot_general(
        value_delta, value_full, contract_last, preferred_element_type=jnp.float32
    ) + lax.dot_general(gate_delta, gate_full, contract_last, preferred_element_type=jnp.float32)
    input_grad = lax.psum_scatter(
        partial_grad.astype(jnp.bfloat16), "mp", scatter_dimension=1, tiled=True
    )
    gated_owned = gated.reshape(1, peers, capacity, -1)
    normed_grad = input_grad.reshape(1, peers, capacity, -1)
    return (gated_owned, value_grad, gate_grad, normed_grad)


def solution(mesh):
    placed = (
        P("dp", "mp"),
        P("dp", None),
        P("dp"),
        P(),
        P("dp", "mp"),
        P("dp", "mp"),
        P("dp", None, None, "mp"),
    )
    return jax.shard_map(
        body,
        mesh=mesh,
        in_specs=placed,
        out_specs=(
            P("dp", None, None, "mp"),
            P("dp", "mp"),
            P("dp", "mp"),
            P("dp", None, None, "mp"),
        ),
        check_vma=False,
    )
```

profile of v0, /device:TPU:0, one launch (start us, length us, event | category | flops | bytes accessed | tf_op | source)
XLA Modules:
  0.0 159.5 jit_solution(10310689362468359501)
XLA Ops:
  7.2 0.0 copy-start
  7.2 0.0 all-gather.5.cloned.1.call-start
  7.2 0.7 all-gather.5.cloned.1.call-update
  7.9 0.7 convert_element_type.64
  8.6 0.9 convert_reduce_fusion.1
  9.5 0.7 multiply_add_fusion
  10.2 0.2 fusion.23
  10.4 0.7 all_to_all.12
  11.1 6.3 %all-to-all-start.1 = ((bf16[8,1,32]{2,1,0:T(2,128)(2,1)}), bf16[8,1,32]{2,1,0:T(2,128)(2,1)S(1)}, u32[]{:S(2)}, u32[]{:S(2)}) async-start(bf16[8,1,32]{2,1,0:T(2,128)(2,1)} %all_to_all.12), calls=%async_computation.1 | async-start | bytes 8192 | tf_op jit(solution)/shard_map/all_to_all | solution.py:61
  17.4 0.0 all-gather.3.cloned.1.call-start
  17.5 0.7 all-gather.3.cloned.1.call-update
  18.2 0.0 copy-done
  18.2 0.9 convolution_convert_fusion
  19.1 0.0 copy-start.4
  19.1 3.8 %all-to-all-done.1 = bf16[8,1,32]{2,1,0:T(2,128)(2,1)S(1)} async-done(((bf16[8,1,32]{2,1,0:T(2,128)(2,1)}), bf16[8,1,32]{2,1,0:T(2,128)(2,1)S(1)}, u32[]{:S(2)}, u32[]{:S(2)}) %all-to-all-start.1) | async-done | bytes 544 | tf_op jit(solution)/shard_map/all_to_all | solution.py:61
  22.9 3.4 %all-to-all-start = ((bf16[8,32,384]{2,1,0:T(8,128)(2,1)}), bf16[8,32,384]{2,1,0:T(8,128)(2,1)S(1)}, u32[]{:S(2)}, u32[]{:S(2)}) async-start(bf16[8,32,384]{2,1,0:T(8,128)(2,1)} %bitcast.1), calls=%async_computation | async-start | bytes 393216 | tf_op jit(solution)/shard_map/all_to_all | solution.py:60
  26.3 0.0 reduce-scatter.7.cloned.1.call-start
  26.4 0.1 reshape.86
  26.5 11.3 %all-to-all-done = bf16[8,32,384]{2,1,0:T(8,128)(2,1)S(1)} async-done(((bf16[8,32,384]{2,1,0:T(8,128)(2,1)}), bf16[8,32,384]{2,1,0:T(8,128)(2,1)S(1)}, u32[]{:S(2)}, u32[]{:S(2)}) %all-to-all-start) | async-done | bytes 196640 | tf_op jit(solution)/shard_map/all_to_all | solution.py:60
  37.8 14.1 %all_gather.9 = bf16[8,32,1536]{2,1,0:T(8,128)(2,1)S(1)} all-gather(bf16[8,32,384]{2,1,0:T(8,128)(2,1)S(1)} %all-to-all-done), channel_id=1, replica_groups=mesh['dp'=8,'mp'=4] {'mp'}, dimensions={2}, use_global_device_ids=true | all-gather | bytes 983040 | tf_op jit(solution)/shard_map/all_gather | solution.py:63
  51.9 0.2 convert_reduce_fusion
  52.1 0.3 fusion.3
  52.4 0.0 copy-done.4
  52.4 0.4 fusion.6
  52.8 0.0 all-gather.5.cloned.1.call-done
  52.9 1.9 %fusion.9 = f32[8,32,384]{2,1,0:T(8,128)S(1)} fusion(bf16[8,32,1536]{2,1,0:T(8,128)(2,1)S(1)} %fusion.6, bf16[1536,384]{1,0:T(8,128)(2,1)} %all-gather.5.cloned.1.call-done), kind=kOutput, calls=%fused_computation.13 | convolution fusion | flops 302284800 | bytes 2359296 | tf_op jit(solution)/shard_map/skd,de->ske/dot_general | solution.py:21
  54.8 0.0 copy-start.3
  54.8 7.9 %all-gather.3.cloned.1.call-done = bf16[1536,384]{1,0:T(8,128)(2,1)} async-done(((bf16[192,384]{1,0:T(8,128)(2,1)}), bf16[1536,384]{1,0:T(8,128)(2,1)}) %all-gather.3.cloned.1.call-update) | async-done | bytes 1179664 | tf_op jit(solution)/shard_map/all_gather | solution.py:56
  62.7 0.0 copy-start.1
  62.7 1.9 %fusion.11 = f32[8,32,384]{2,1,0:T(8,128)S(1)} fusion(bf16[8,32,1536]{2,1,0:T(8,128)(2,1)S(1)} %fusion.6, bf16[1536,384]{1,0:T(8,128)(2,1)} %all-gather.3.cloned.1.call-done), kind=kOutput, calls=%fused_computation.15 | convolution fusion | flops 301989888 | bytes 2359296 | tf_op jit(solution)/shard_map/skd,de->ske/dot_general | solution.py:20
  64.6 0.0 copy-done.3
  64.7 0.1 fusion.14
  64.8 0.0 copy-start.2
  64.8 0.0 copy-done.1
  64.8 0.6 fusion.29
  65.4 0.6 copy-done.2
  66.1 0.6 fusion
  66.7 1.2 copy.13
  67.9 0.0 reduce-scatter.7.cloned.1.call-update
  67.9 0.0 reduce-scatter.5.cloned.1.call-start
  68.0 3.0 %fusion.19 = f32[1536,768]{1,0:T(8,128)} fusion(bf16[256,1536]{1,0:T(8,128)(2,1)S(1)} %bitcast.37, bf16[256,384]{1,0:T(8,128)(2,1)S(1)} %get-tuple-element.5, bf16[256,384]{1,0:T(8,128)(2,1)S(1)} %get-tuple-element.4), kind=kOutput, calls=%fused_computation.26 | convolution fusion | flops 604766208 | bytes 5898240 | tf_op jit(solution)/shard_map/dot_general | solution.py:26
  70.9 0.0 reduce-scatter.5.cloned.1.call-update
  70.9 0.7 fusion.24
  71.7 22.3 %reduce-scatter.7.cloned.1.call-done = bf16[384,256]{1,0:T(8,128)(2,1)} async-done(((bf16[1536,256]{1,0:T(8,128)(2,1)}), bf16[384,256]{1,0:T(8,128)(2,1)}) %reduce-scatter.7.cloned.1.call-update) | async-done | bytes 196624
  93.9 1.7 %copy.14 = bf16[256,384]{1,0:T(8,128)(2,1)} copy(bf16[256,384]{0,1:T(8,128)(2,1)} %bitcast.39) | data formatting | bytes 393216
  95.7 55.4 %reduce-scatter.5.cloned.1.call-done = f32[192,768]{1,0:T(8,128)} async-done(((f32[1536,768]{1,0:T(8,128)}), f32[192,768]{1,0:T(8,128)}) %reduce-scatter.5.cloned.1.call-update) | async-done | bytes 589840 | tf_op jit(solution)/shard_map/reduce_scatter | solution.py:79
  151.1 1.9 %slice_multiply_fusion = (f32[192,384]{1,0:T(8,128)}, f32[192,384]{1,0:T(8,128)}) fusion(f32[192,768]{1,0:T(8,128)} %reduce-scatter.5.cloned.1.call-done), kind=kLoop, calls=%fused_computation.32 | loop fusion | flops 147456 | bytes 1179648 | tf_op jit(solution)/shard_map/mul | solution.py:84
  (6 shorter events, 0.0 us)
Async XLA Ops:
  7.2 11.0 %copy-start = (bf16[192,384]{1,0:T(8,128)(2,1)S(1)}, bf16[192,384]{1,0:T(8,128)(2,1)}, u32[]{:S(2)}) copy-start(bf16[192,384]{1,0:T(8,128)(2,1)} %param.7) | copy-start | bytes 442372
  7.2 45.7 %all-gather.5.cloned.1.call-start = ((), (), s32[]{:S(2)}) async-start(), calls=%async_computation.5 | async-start | bytes 1327104 | tf_op jit(solution)/shard_map/all_gather | solution.py:57
  11.1 11.8 %all-to-all-start.1 = ((bf16[8,1,32]{2,1,0:T(2,128)(2,1)}), bf16[8,1,32]{2,1,0:T(2,128)(2,1)S(1)}, u32[]{:S(2)}, u32[]{:S(2)}) async-start(bf16[8,1,32]{2,1,0:T(2,128)(2,1)} %all_to_all.12), calls=%async_computation.1 | async-start | bytes 8192 | tf_op jit(solution)/shard_map/all_to_all | solution.py:61
  17.4 45.3 %all-gather.3.cloned.1.call-start = ((), (), s32[]{:S(2)}) async-start(), calls=%async_computation.4 | async-start | bytes 1327104 | tf_op jit(solution)/shard_map/all_gather | solution.py:56
  19.1 33.3 %copy-start.4 = (f32[1536]{0:T(1024)S(1)}, f32[1536]{0:T(1024)}, u32[]{:S(2)}) copy-start(f32[1536]{0:T(1024)} %param.10) | copy-start | bytes 18436
  22.9 14.9 %all-to-all-start = ((bf16[8,32,384]{2,1,0:T(8,128)(2,1)}), bf16[8,32,384]{2,1,0:T(8,128)(2,1)S(1)}, u32[]{:S(2)}, u32[]{:S(2)}) async-start(bf16[8,32,384]{2,1,0:T(8,128)(2,1)} %bitcast.1), calls=%async_computation | async-start | bytes 393216 | tf_op jit(solution)/shard_map/all_to_all | solution.py:60
  26.3 67.6 %reduce-scatter.7.cloned.1.call-start = ((), (), s32[]{:S(2)}) async-start(), calls=%async_computation.7 | async-start | bytes 983040
  54.8 9.9 %copy-start.3 = (bf16[1,8,32,384]{3,2,1,0:T(8,128)(2,1)S(1)}, bf16[1,8,32,384]{3,2,1,0:T(8,128)(2,1)}, u32[]{:S(2)}) copy-start(bf16[1,8,32,384]{3,2,1,0:T(8,128)(2,1)} %param.13) | copy-start | bytes 589828
  62.7 2.1 %copy-start.1 = (bf16[1536,384]{1,0:T(8,128)(2,1)S(1)}, bf16[1536,384]{1,0:T(8,128)(2,1)}, u32[]{:S(2)}) copy-start(bf16[1536,384]{1,0:T(8,128)(2,1)} %all-gather.3.cloned.1.call-done) | copy-start | bytes 3538948
  64.8 1.3 copy-start.2
  67.9 83.2 %reduce-scatter.5.cloned.1.call-start = ((), (), s32[]{:S(2)}) async-start(), calls=%async_computation.6 | async-start | bytes 5308416 | tf_op jit(solution)/shard_map/reduce_scatter | solution.py:79
Sparse Core Ops, SparseCore 0:
  9.7 29.4 all-gather.4
  40.8 21.8 all-gather.2
  68.0 25.8 reduce-scatter.6
  96.1 54.9 reduce-scatter.4
where the time goes:
time: 160 us
  waiting for transfers between devices  102 us (64%)
  blocking collectives  14.1 us (9%)
  between operations  13.9 us (9%)
  starting transfers between devices  9.88 us (6%)
  matrix products  9.09 us (6%)
  other arithmetic  6.05 us (4%)
  local copies, waits for them, and re-layouts  4.37 us (3%)
    reduce_scatter x1, waiting for transfers between devices, body(): lax.psum_scatter(column_term(normed_flat, both_delta), 'dp', scatter_dime...  55.4 us
    unnamed x5, waiting for transfers between devices  23.7 us
    all_gather x1, blocking collectives, body(): whole = lax.all_gather(received_rows, 'mp', axis=2, tiled=True)  14.1 us
    all_to_all x1, waiting for transfers between devices, body(): lax.all_to_all(send_buffer, 'dp', split_axis=0, concat_axis=0, tiled=True)  11.3 us
    all_gather x1, waiting for transfers between devices, body(): lax.all_gather(value_weight, 'dp', axis=0, tiled=True)  7.92 us
    all_to_all x1, starting transfers between devices, body(): lax.all_to_all(send_live, 'dp', split_axis=0, concat_axis=0, tiled=True)  6.33 us
    all_to_all x1, waiting for transfers between devices, body(): lax.all_to_all(send_live, 'dp', split_axis=0, concat_axis=0, tiled=True)  3.81 us
    unnamed x12, local copies, waits for them, and re-layouts  3.58 us
  transfers between devices with their start and end apart: 6, of which 5 were waited for; matrix products, arithmetic and copies ran while one was open for 7% of the time, Pallas kernels for 0%

commit v1 on v0

--- a/solution.py
+++ b/solution.py
@@ -1,6 +1,9 @@
+import functools
 import jax
 import jax.numpy as jnp
 from jax import lax
+from jax.experimental import pallas as pl
+from jax.experimental.pallas import tpu as pltpu
 from jax.sharding import PartitionSpec as P
 
 epsilon = 1e-05
@@ -28,7 +31,7 @@
     )
 
 
-def body(frames, frame_owner, frame_valid, norm_gain, value_weight, gate_weight, grad_owned):
+def plain_body(frames, frame_owner, frame_valid, norm_gain, value_weight, gate_weight, grad_owned):
     peers = lax.axis_size("dp")
     capacity = grad_owned.shape[2]
     row_total = frames.shape[0]
@@ -94,6 +97,374 @@
     return (gated_owned, value_grad, gate_grad, normed_grad)
 
 
+filler = 65536.0
+MESH = pl.DeviceIdType.MESH
+
+
+def kernel(
+    peers, groups, capacity, scale,
+    frames_ref, owner_ref, valid_ref, gain_ref, value_ref, gate_ref, upstream_ref,
+    gated_ref, value_grad_ref, gate_grad_ref, input_grad_ref,
+    outgoing, whole, weights, normed, normed_t, sibling_t, delta, sibling_delta,
+    from_below, from_above, to_above, to_below, term_out, term_in,
+    rows_send, rows_recv, mp_send, mp_recv, w_up, w_down, w_side, w_recv,
+    t_send, t_recv, d_send, d_recv, up_send, up_recv, down_send, down_recv, x_send, x_recv,
+):
+    me, column = lax.axis_index("dp"), lax.axis_index("mp")
+    chips = peers // 2
+    chip, core = me // 2, me % 2
+    twin = chip * 2 + 1 - core
+    above, below = me + 2, me - 2
+    loaded, width = frames_ref.shape
+    slots = peers * capacity
+    depth = value_ref.shape[0]
+    channels = width * groups
+    inner, last = chip > 0, chip < chips - 1
+
+    barrier = pltpu.get_barrier_semaphore()
+    for step in range(1, peers):
+        pl.semaphore_signal(
+            barrier, inc=1, device_id={"dp": lax.rem(me + step, peers)}, device_id_type=MESH
+        )
+    for step in range(1, groups):
+        pl.semaphore_signal(
+            barrier, inc=1, device_id={"mp": lax.rem(column + step, groups)}, device_id_type=MESH
+        )
+
+    owner = owner_ref[...]
+    lanes = -(-peers // 128) * 128
+    named = (lax.broadcasted_iota(jnp.int32, (loaded, lanes), 1) == owner).astype(jnp.float32)
+    first = lax.broadcasted_iota(jnp.int32, (loaded, loaded), 0)
+    second = lax.broadcasted_iota(jnp.int32, (loaded, loaded), 1)
+    counts = jnp.dot(
+        (second < first).astype(jnp.bfloat16), named.astype(jnp.bfloat16),
+        preferred_element_type=jnp.float32,
+    )
+    slot = jnp.sum(named * counts, axis=1, keepdims=True)
+    target = owner.astype(jnp.float32) * capacity + slot
+    target_row = jnp.sum(jnp.where(first == second, target, 0.0), axis=0, keepdims=True)
+    placing = lax.broadcasted_iota(jnp.int32, (slots, loaded), 0) == target_row.astype(jnp.int32)
+    present = jnp.sum(
+        jnp.where(placing, valid_ref[...].astype(jnp.float32), 0.0), axis=1, keepdims=True
+    )
+    placed = jnp.dot(
+        placing.astype(jnp.bfloat16), frames_ref[...], preferred_element_type=jnp.float32
+    )
+    outgoing[...] = (
+        jnp.where(present > 0.5, placed, filler).astype(jnp.bfloat16).reshape(outgoing.shape)
+    )
+
+    pl.semaphore_wait(barrier, peers - 1 + groups - 1)
+
+    def remote(src, dst, send, recv, **device):
+        return pltpu.make_async_remote_copy(
+            src_ref=src, dst_ref=dst, send_sem=send, recv_sem=recv,
+            device_id=device, device_id_type=MESH,
+        )
+
+    def rows_copy(step):
+        peer = lax.rem(me + step, peers)
+        return remote(
+            outgoing.at[peer], whole.at[column, me], rows_send.at[peer], rows_recv.at[me], dp=peer
+        )
+
+    def rows_arrival(step):
+        peer = lax.rem(me + step, peers)
+        return remote(
+            outgoing.at[peer], whole.at[column, peer], rows_send.at[peer], rows_recv.at[peer], dp=peer
+        )
+
+    for step in range(1, peers):
+        rows_copy(step).start()
+    whole[column, me] = outgoing[me]
+
+    def part(shard, half):
+        return weights.at[pl.ds(pl.multiple_of(shard * depth, depth), depth), pl.ds(half * width, width)]
+
+    def weight_copy(where, source, half, peer):
+        shard = source * 2 + core
+        return remote(
+            part(shard, half), part(shard, half), where.at[source, half], w_recv.at[shard, half],
+            dp=peer,
+        )
+
+    def weight_arrival(shard, half):
+        return remote(
+            part(shard, half), part(shard, half), w_side.at[0, half], w_recv.at[shard, half], dp=twin
+        )
+
+    for half, ref in enumerate((value_ref, gate_ref)):
+        weights[pl.ds(pl.multiple_of(me * depth, depth), depth), half * width:(half + 1) * width] = ref[...]
+    for half in range(2):
+        pl.when(last)(lambda: weight_copy(w_up, chip, half, above).start())
+        pl.when(inner)(lambda: weight_copy(w_down, chip, half, below).start())
+    for half in range(2):
+        weight_copy(w_side, chip, half, twin).start()
+
+    def relay(step):
+        for half in range(2):
+            @pl.when(chip >= step)
+            def _():
+                source = chip - step
+                weight_arrival(source * 2 + core, half).wait_recv()
+                pl.when(last)(lambda: weight_copy(w_up, source, half, above).start())
+                weight_copy(w_side, source, half, twin).start()
+
+            @pl.when(chip + step < chips)
+            def _():
+                source = chip + step
+                weight_arrival(source * 2 + core, half).wait_recv()
+                pl.when(inner)(lambda: weight_copy(w_down, source, half, below).start())
+                weight_copy(w_side, source, half, twin).start()
+
+    for step in range(1, peers):
+        rows_arrival(step).wait_recv()
+
+    def mp_copy(step):
+        peer = lax.rem(column + step, groups)
+        return remote(whole.at[column], whole.at[column], mp_send.at[peer], mp_recv.at[column], mp=peer)
+
+    def mp_arrival(step):
+        peer = lax.rem(column + step, groups)
+        return remote(whole.at[peer], whole.at[peer], mp_send.at[peer], mp_recv.at[peer], mp=peer)
+
+    for step in range(1, groups):
+        mp_copy(step).start()
+    early = min(2, chips - 1)
+    for step in range(1, early + 1):
+        relay(step)
+    for step in range(1, groups):
+        mp_arrival(step).wait_recv()
+
+    def block(group):
+        return whole[group].reshape(slots, width).astype(jnp.float32)
+
+    live = block(0)[:, :1] < 0.5 * filler
+    live_col = live.astype(jnp.float32)
+    total = jnp.zeros((slots, 1), jnp.float32)
+    for group in range(groups):
+        total += jnp.sum(block(group), axis=1, keepdims=True)
+    row_mean = jnp.where(live, total / channels, 0.0)
+    square = jnp.zeros((slots, 1), jnp.float32)
+    for group in range(groups):
+        centred = jnp.where(live, block(group) - row_mean, 0.0)
+        square += jnp.sum(centred * centred, axis=1, keepdims=True)
+    factor = lax.rsqrt(square / channels + epsilon)
+    for group in range(groups):
+        at = slice(group * width, (group + 1) * width)
+        centred = jnp.where(live, block(group) - row_mean, 0.0)
+        wide = centred * factor * gain_ref[:, at] * live_col
+        normed[:, at] = wide.astype(jnp.bfloat16)
+        normed_t[at, :] = wide.T.astype(jnp.bfloat16)
+
+    def rows_of(shard):
+        return pl.ds(pl.multiple_of(shard * depth, depth), depth)
+
+    def t_copy(target):
+        return remote(
+            normed_t.at[rows_of(target * 2 + 1 - core)], sibling_t.at[target],
+            t_send.at[target], t_recv.at[target], dp=twin,
+        )
+
+    for target in range(chips):
+        t_copy(target).start()
+    for step in range(early + 1, chips):
+        relay(step)
+    for step in range(chips):
+        for half in range(2):
+            weight_arrival(step * 2 + 1 - core, half).wait_recv()
+
+    act = jnp.dot(normed[...], weights[...], preferred_element_type=jnp.float32)
+    value_act = act[:, :width]
+    gate_sig = jax.nn.sigmoid(act[:, width:])
+    upstream = upstream_ref[...].astype(jnp.float32)
+    gated_ref[...] = (value_act * gate_sig).astype(jnp.bfloat16)
+    delta[:, :width] = (upstream * gate_sig * live_col).astype(jnp.bfloat16)
+    delta[:, width:] = (upstream * value_act * gate_sig * (1.0 - gate_sig) * live_col).astype(
+        jnp.bfloat16
+    )
+    delta_copy = remote(delta, sibling_delta, d_send.at[0], d_recv.at[0], dp=twin)
+    delta_copy.start()
+
+    def term(group):
+        rows = weights[pl.ds(pl.multiple_of(group * width, width), width), :]
+        return lax.dot_general(
+            delta[...], rows, (((1,), (1,)), ((), ())), preferred_element_type=jnp.float32
+        ).astype(jnp.bfloat16)
+
+    def x_copy(step):
+        peer = lax.rem(column + step, groups)
+        return remote(term_out.at[peer], term_in.at[column], x_send.at[peer], x_recv.at[column], mp=peer)
+
+    def x_arrival(step):
+        peer = lax.rem(column + step, groups)
+        return remote(term_out.at[peer], term_in.at[peer], x_send.at[peer], x_recv.at[peer], mp=peer)
+
+    for step in range(1, groups):
+        peer = lax.rem(column + step, groups)
+        term_out[peer] = term(peer)
+        x_copy(step).start()
+
+    delta_copy.wait_recv()
+    for target in range(chips):
+        t_copy(target).wait_recv()
+
+    def chip_sum(target):
+        return jnp.dot(
+            normed_t[rows_of(target * 2 + core), :], delta[...], preferred_element_type=jnp.float32
+        ) + jnp.dot(sibling_t[target], sibling_delta[...], preferred_element_type=jnp.float32)
+
+    def up_copy(target):
+        return remote(
+            to_above.at[target], from_below.at[target], up_send.at[target], up_recv.at[target], dp=above
+        )
+
+    def up_arrival(target):
+        return remote(
+            to_above.at[target], from_below.at[target], up_send.at[target], up_recv.at[target], dp=below
+        )
+
+    def down_copy(target):
+        return remote(
+            to_below.at[target], from_above.at[target], down_send.at[target], down_recv.at[target], dp=below
+        )
+
+    def down_arrival(target):
+        return remote(
+            to_below.at[target], from_above.at[target], down_send.at[target], down_recv.at[target], dp=above
+        )
+
+    for step in range(chips - 1, 0, -1):
+        @pl.when(chip + step < chips)
+        def _():
+            target = chip + step
+            own = chip_sum(target)
+
+            @pl.when(inner)
+            def _():
+                up_arrival(target).wait_recv()
+                to_above[target] = (own + from_below[target].astype(jnp.float32)).astype(jnp.bfloat16)
+
+            @pl.when(jnp.logical_not(inner))
+            def _():
+                to_above[target] = own.astype(jnp.bfloat16)
+
+            up_copy(target).start()
+
+        @pl.when(chip >= step)
+        def _():
+            target = chip - step
+            own = chip_sum(target)
+
+            @pl.when(last)
+            def _():
+                down_arrival(target).wait_recv()
+                to_below[target] = (own + from_above[target].astype(jnp.float32)).astype(jnp.bfloat16)
+
+            @pl.when(jnp.logical_not(last))
+            def _():
+                to_below[target] = own.astype(jnp.bfloat16)
+
+            down_copy(target).start()
+
+    own = chip_sum(chip)
+    value_grad_ref[...] = own[:, :width]
+    gate_grad_ref[...] = own[:, width:]
+
+    input_grad = term(column).astype(jnp.float32)
+    for step in range(1, groups):
+        x_arrival(step).wait_recv()
+        input_grad += term_in[lax.rem(column + step, groups)].astype(jnp.float32)
+    input_grad_ref[...] = input_grad.astype(jnp.bfloat16)
+
+    def add(arrived):
+        value_grad_ref[...] += arrived[chip][:, :width].astype(jnp.float32)
+        gate_grad_ref[...] += arrived[chip][:, width:].astype(jnp.float32)
+
+    @pl.when(inner)
+    def _():
+        up_arrival(chip).wait_recv()
+        add(from_below)
+
+    @pl.when(last)
+    def _():
+        down_arrival(chip).wait_recv()
+        add(from_above)
+
+    value_grad_ref[...] *= scale
+    gate_grad_ref[...] *= scale
+
+    for step in range(1, peers):
+        rows_copy(step).wait_send()
+    for step in range(1, groups):
+        mp_copy(step).wait_send()
+        x_copy(step).wait_send()
+    delta_copy.wait_send()
+    for source in range(chips):
+        t_copy(source).wait_send()
+        for half in range(2):
+            weight_copy(w_side, source, half, twin).wait_send()
+            pl.when(last & (source <= chip))(lambda: weight_copy(w_up, source, half, above).wait_send())
+            pl.when(inner & (source >= chip))(lambda: weight_copy(w_down, source, half, below).wait_send())
+        pl.when(source > chip)(lambda: up_copy(source).wait_send())
+        pl.when(source < chip)(lambda: down_copy(source).wait_send())
+
+
+def body(frames, frame_owner, frame_valid, norm_gain, value_weight, gate_weight, grad_owned):
+    peers, groups = lax.axis_size("dp"), lax.axis_size("mp")
+    capacity = grad_owned.shape[2]
+    loaded, width = frames.shape
+    depth = value_weight.shape[0]
+    if peers % 2 or depth % 16 or capacity % 16 or loaded % 16 or width % 128 or groups * width != peers * depth:
+        return plain_body(
+            frames, frame_owner, frame_valid, norm_gain, value_weight, gate_weight, grad_owned
+        )
+    slots, chips, channels = peers * capacity, peers // 2, width * groups
+    half, full = jnp.bfloat16, jnp.float32
+    dma = pltpu.SemaphoreType.DMA
+    hop = pltpu.VMEM((chips, depth, 2 * width), half)
+    vmem = pl.BlockSpec(memory_space=pltpu.VMEM)
+    gated, value_grad, gate_grad, input_grad = pl.pallas_call(
+        functools.partial(kernel, peers, groups, capacity, float(loaded * peers) ** (-0.5)),
+        out_shape=(
+            jax.ShapeDtypeStruct((slots, width), half),
+            jax.ShapeDtypeStruct((depth, width), full),
+            jax.ShapeDtypeStruct((depth, width), full),
+            jax.ShapeDtypeStruct((slots, width), half),
+        ),
+        in_specs=[vmem] * 7,
+        out_specs=(vmem,) * 4,
+        scratch_shapes=[
+            pltpu.VMEM((peers, capacity, width), half),
+            pltpu.VMEM((groups, peers, capacity, width), half),
+            pltpu.VMEM((channels, 2 * width), half),
+            pltpu.VMEM((slots, channels), half),
+            pltpu.VMEM((channels, slots), half),
+            pltpu.VMEM((chips, depth, slots), half),
+            pltpu.VMEM((slots, 2 * width), half),
+            pltpu.VMEM((slots, 2 * width), half),
+            hop, hop, hop, hop,
+            pltpu.VMEM((groups, slots, width), half),
+            pltpu.VMEM((groups, slots, width), half),
+            dma((peers,)), dma((peers,)), dma((groups,)), dma((groups,)),
+            dma((chips, 2)), dma((chips, 2)), dma((chips, 2)), dma((peers, 2)),
+            dma((chips,)), dma((chips,)), dma((1,)), dma((1,)),
+            dma((chips,)), dma((chips,)), dma((chips,)), dma((chips,)),
+            dma((groups,)), dma((groups,)),
+        ],
+        compiler_params=pltpu.CompilerParams(
+            collective_id=0, has_side_effects=True, vmem_limit_bytes=48 * 1024 * 1024
+        ),
+    )(
+        frames, frame_owner, frame_valid.reshape(1, loaded), norm_gain.reshape(1, channels),
+        value_weight, gate_weight, grad_owned.reshape(slots, width),
+    )
+    return (
+        gated.reshape(1, peers, capacity, width), value_grad, gate_grad,
+        input_grad.reshape(1, peers, capacity, width),
+    )
+
+
 def solution(mesh):
     placed = (
         P("dp", "mp"),

time: 160 us -> 65.5 us (0.41)
  waiting for transfers between devices: 102 us -> 0 us
  Pallas kernels: 0 us -> 56.7 us
  blocking collectives: 14.1 us -> 0 us
  between operations: 13.9 us -> 0.67 us
  starting transfers between devices: 9.88 us -> 0 us
  matrix products: 9.09 us -> 0 us
  other arithmetic: 6.05 us -> 0 us
  local copies, waits for them, and re-layouts: 4.37 us -> 7.82 us
    pallas_call x0 -> x1, Pallas kernels: none -> 56.7 us  [body(): pl.pallas_call(functools.partial(kernel, peers, groups, capacity, float(l...]
    reduce_scatter x1 -> x0, waiting for transfers between devices: 55.4 us -> none  [body(): lax.psum_scatter(column_term(normed_flat, both_delta), 'dp', scatter_dime...]
    unnamed x5 -> x0, waiting for transfers between devices: 23.7 us -> none
    all_to_all x2 -> x0, waiting for transfers between devices: 15.1 us -> none  [the longest x1 11.3 us: body(): lax.all_to_all(send_buffer, 'dp', split_axis=0, concat_axis=0, tiled=True)]
    all_gather x1 -> x0, blocking collectives: 14.1 us -> none  [body(): whole = lax.all_gather(received_rows, 'mp', axis=2, tiled=True)]
    all_to_all x2 -> x0, starting transfers between devices: 9.72 us -> none  [the longest x1 6.33 us: body(): lax.all_to_all(send_live, 'dp', split_axis=0, concat_axis=0, tiled=True)]
    dot_general x7 -> x0, matrix products: 9.09 us -> none  [the longest x1 2.96 us: column_term(): lax.dot_general(normed_flat, delta, (((0,), (0,)), ((), ())), preferred_e...]
    all_gather x2 -> x0, waiting for transfers between devices: 7.94 us -> none  [the longest x1 7.92 us: body(): lax.all_gather(value_weight, 'dp', axis=0, tiled=True)]
  transfers between devices with their start and end apart: 6 -> 0, of which waited for: 5 -> 0; matrix products, arithmetic and copies ran while one was open for 7% -> 0% of each run, Pallas kernels for 0% -> 0%
where the time goes in v1:
time: 65.5 us; the launch traced here: 65.2 us
  Pallas kernels  56.7 us (87%)
  local copies, waits for them, and re-layouts  7.82 us (12%)
  between operations  0.67 us (1%)
    pallas_call x1, Pallas kernels, body(): pl.pallas_call(functools.partial(kernel, peers, groups, capacity, float(l...  56.7 us
    unnamed x17, local copies, waits for them, and re-layouts  7.11 us

profile of v1, /device:TPU:0, one launch (start us, length us, event | category | flops | bytes accessed | tf_op | source)
XLA Modules:
  0.0 65.2 jit_solution(13222782690616037173)
XLA Ops:
  0.6 0.0 copy-start.5
  0.6 0.7 %reshape.24.gain_ref = f32[1,1536]{1,0:T(1,128)S(1)} reshape(f32[1536]{0:T(1024)} %param.10) | data formatting | bytes 12288 | tf_op jit(solution)/shard_map/reshape | solution.py:459
  1.3 0.0 copy-done.5
  1.4 0.0 copy-start.4
  1.4 0.1 copy.11.owner_ref
  1.5 0.6 copy-done.4
  2.0 0.0 copy-start
  2.0 0.9 %copy-done = bf16[1,8,32,384]{3,2,1,0:T(8,128)(2,1)S(1)} copy-done((bf16[1,8,32,384]{3,2,1,0:T(8,128)(2,1)S(1)}, bf16[1,8,32,384]{3,2,1,0:T(8,128)(2,1)}, u32[]{:S(2)}) %copy-start) | copy-done | bytes 196632
  3.0 0.0 copy-start.1
  3.0 0.9 %copy-done.1 = bf16[192,384]{1,0:T(8,128)(2,1)S(1)} copy-done((bf16[192,384]{1,0:T(8,128)(2,1)S(1)}, bf16[192,384]{1,0:T(8,128)(2,1)}, u32[]{:S(2)}) %copy-start.1) | copy-done | bytes 147480
  3.9 0.0 copy-start.2
  3.9 0.9 %copy-done.2 = bf16[192,384]{1,0:T(8,128)(2,1)S(1)} copy-done((bf16[192,384]{1,0:T(8,128)(2,1)S(1)}, bf16[192,384]{1,0:T(8,128)(2,1)}, u32[]{:S(2)}) %copy-start.2) | copy-done | bytes 147480
  4.8 0.0 copy-start.3
  4.8 0.9 %copy-done.3 = bf16[192,384]{1,0:T(8,128)(2,1)S(1)} copy-done((bf16[192,384]{1,0:T(8,128)(2,1)S(1)}, bf16[192,384]{1,0:T(8,128)(2,1)}, u32[]{:S(2)}) %copy-start.3) | copy-done | bytes 147480
  5.7 56.7 %shard_map.102 = (bf16[256,384]{1,0:T(8,128)(2,1)S(1)}, f32[192,384]{1,0:T(8,128)S(1)}, f32[192,384]{1,0:T(8,128)S(1)}, bf16[256,384]{1,0:T(8,128)(2,1)S(1)}) custom-call(bf16[192,384]{1,0:T(8,128)(2,1)S(1)} %copy-done.1, s32[192,1]{1,0:T(8,128)S(1)} %copy.11.owner_ref, s32[1,192]{1,0:T(1,128)S(1)} %bitcast.7, f32[1,1536]{1,0:T(1,128)S(1)} %reshape.24.gain_ref, ...), custom_call_target="tpu_custom_call" | custom-call | tf_op jit(solution)/shard_map/pallas_call | solution.py:427
  62.4 0.7 %copy.16 = bf16[1,8,32,384]{3,2,1,0:T(8,128)(2,1)} copy(bf16[1,8,32,384]{3,2,1,0:T(8,128)(2,1)S(1)} %bitcast.5) | data formatting | bytes 393216
  63.1 0.7 %copy.17 = f32[192,384]{1,0:T(8,128)} copy(f32[192,384]{1,0:T(8,128)S(1)} %get-tuple-element.17) | data formatting | bytes 589824
  63.8 0.7 %copy.18 = f32[192,384]{1,0:T(8,128)} copy(f32[192,384]{1,0:T(8,128)S(1)} %get-tuple-element.18) | data formatting | bytes 589824
  64.5 0.7 %copy.19 = bf16[1,8,32,384]{3,2,1,0:T(8,128)(2,1)} copy(bf16[1,8,32,384]{3,2,1,0:T(8,128)(2,1)S(1)} %bitcast.4) | data formatting | bytes 393216
Async XLA Ops:
  0.6 0.7 %copy-start.5 = (s32[192,1]{0,1:T(1,128)S(1)}, s32[192,1]{0,1:T(1,128)}, u32[]{:S(2)}) copy-start(s32[192,1]{0,1:T(1,128)} %param.8) | copy-start | bytes 2308
  1.4 0.7 %copy-start.4 = (s32[192]{0:T(256)S(1)}, s32[192]{0:T(256)}, u32[]{:S(2)}) copy-start(s32[192]{0:T(256)} %param.9) | copy-start | bytes 2308
  2.0 0.9 %copy-start = (bf16[1,8,32,384]{3,2,1,0:T(8,128)(2,1)S(1)}, bf16[1,8,32,384]{3,2,1,0:T(8,128)(2,1)}, u32[]{:S(2)}) copy-start(bf16[1,8,32,384]{3,2,1,0:T(8,128)(2,1)} %param.13) | copy-start | bytes 589828
  3.0 0.9 %copy-start.1 = (bf16[192,384]{1,0:T(8,128)(2,1)S(1)}, bf16[192,384]{1,0:T(8,128)(2,1)}, u32[]{:S(2)}) copy-start(bf16[192,384]{1,0:T(8,128)(2,1)} %frames_ref.1) | copy-start | bytes 442372
  3.9 0.9 %copy-start.2 = (bf16[192,384]{1,0:T(8,128)(2,1)S(1)}, bf16[192,384]{1,0:T(8,128)(2,1)}, u32[]{:S(2)}) copy-start(bf16[192,384]{1,0:T(8,128)(2,1)} %value_ref.1) | copy-start | bytes 442372
  4.8 0.9 %copy-start.3 = (bf16[192,384]{1,0:T(8,128)(2,1)S(1)}, bf16[192,384]{1,0:T(8,128)(2,1)}, u32[]{:S(2)}) copy-start(bf16[192,384]{1,0:T(8,128)(2,1)} %gate_ref.1) | copy-start | bytes 442372

commit v2 on v0

--- a/solution.py
+++ b/solution.py
@@ -1,6 +1,9 @@
+import functools
 import jax
 import jax.numpy as jnp
 from jax import lax
+from jax.experimental import pallas as pl
+from jax.experimental.pallas import tpu as pltpu
 from jax.sharding import PartitionSpec as P
 
 epsilon = 1e-05
@@ -28,7 +31,7 @@
     )
 
 
-def body(frames, frame_owner, frame_valid, norm_gain, value_weight, gate_weight, grad_owned):
+def plain_body(frames, frame_owner, frame_valid, norm_gain, value_weight, gate_weight, grad_owned):
     peers = lax.axis_size("dp")
     capacity = grad_owned.shape[2]
     row_total = frames.shape[0]
@@ -94,6 +97,438 @@
     return (gated_owned, value_grad, gate_grad, normed_grad)
 
 
+filler = 65536.0
+MESH = pl.DeviceIdType.MESH
+
+
+def kernel(
+    peers, groups, capacity, scale,
+    frames_ref, owner_ref, valid_ref, gain_ref, value_ref, gate_ref, upstream_ref,
+    gated_ref, value_grad_ref, gate_grad_ref, input_grad_ref,
+    frames_in, owner_in, valid_in, gain_in, upstream_in, outgoing, whole, weights, normed, normed_t, sibling_t, delta, sibling_delta,
+    from_below, from_above, to_above, to_below, term_out, term_in,
+    in_sem, rows_send, rows_recv, mp_send, mp_recv, w_up, w_down, w_side, w_recv,
+    t_send, t_recv, d_send, d_recv, up_send, up_recv, down_send, down_recv, x_send, x_recv,
+):
+    me, column = lax.axis_index("dp"), lax.axis_index("mp")
+    chips = peers // 2
+    chip, core = me // 2, me % 2
+    twin = chip * 2 + 1 - core
+    above, below = me + 2, me - 2
+    loaded, width = frames_ref.shape
+    cuts = width // 128
+    pair = 2 * 128
+    slots = peers * capacity
+    depth = value_ref.shape[0]
+    channels = width * groups
+    inner, last = chip > 0, chip < chips - 1
+
+    barrier = pltpu.get_barrier_semaphore()
+    for step in range(1, peers):
+        pl.semaphore_signal(
+            barrier, inc=1, device_id={"dp": lax.rem(me + step, peers)}, device_id_type=MESH
+        )
+    for step in range(1, groups):
+        pl.semaphore_signal(
+            barrier, inc=1, device_id={"mp": lax.rem(column + step, groups)}, device_id_type=MESH
+        )
+
+    loads = []
+    for ref, held in (
+        (owner_ref, owner_in), (valid_ref, valid_in), (frames_ref, frames_in), (gain_ref, gain_in),
+        (upstream_ref, upstream_in),
+    ):
+        loads.append(pltpu.make_async_copy(ref, held, in_sem.at[len(loads)]))
+    own_rows = pl.ds(pl.multiple_of(me * depth, depth), depth)
+    for cut in range(cuts):
+        for side, ref in enumerate((value_ref, gate_ref)):
+            loads.append(
+                pltpu.make_async_copy(
+                    ref.at[:, pl.ds(cut * 128, 128)],
+                    weights.at[cut, own_rows, pl.ds(side * 128, 128)],
+                    in_sem.at[len(loads)],
+                )
+            )
+    for load in loads:
+        load.start()
+    for load in loads[:3]:
+        load.wait()
+
+    first = lax.broadcasted_iota(jnp.int32, (loaded, loaded), 0)
+    second = lax.broadcasted_iota(jnp.int32, (loaded, loaded), 1)
+    owner = jnp.sum(
+        jnp.where(first == second, owner_in[...].astype(jnp.float32), 0.0), axis=1, keepdims=True
+    )
+    lanes = -(-peers // 128) * 128
+    named = (lax.broadcasted_iota(jnp.int32, (loaded, lanes), 1) == owner.astype(jnp.int32)).astype(
+        jnp.float32
+    )
+    counts = jnp.dot(
+        (second < first).astype(jnp.bfloat16), named.astype(jnp.bfloat16),
+        preferred_element_type=jnp.float32,
+    )
+    slot = jnp.sum(named * counts, axis=1, keepdims=True)
+    target = owner * capacity + slot
+    target_row = jnp.sum(jnp.where(first == second, target, 0.0), axis=0, keepdims=True)
+    placing = lax.broadcasted_iota(jnp.int32, (slots, loaded), 0) == target_row.astype(jnp.int32)
+    present = jnp.sum(
+        jnp.where(placing, valid_in[...].astype(jnp.float32), 0.0), axis=1, keepdims=True
+    )
+    placed = jnp.dot(
+        placing.astype(jnp.bfloat16), frames_in[...], preferred_element_type=jnp.float32
+    )
+    outgoing[...] = (
+        jnp.where(present > 0.5, placed, filler).astype(jnp.bfloat16).reshape(outgoing.shape)
+    )
+
+    pl.semaphore_wait(barrier, peers - 1 + groups - 1)
+
+    def remote(src, dst, send, recv, **device):
+        return pltpu.make_async_remote_copy(
+            src_ref=src, dst_ref=dst, send_sem=send, recv_sem=recv,
+            device_id=device, device_id_type=MESH,
+        )
+
+    def rows_copy(step):
+        peer = lax.rem(me + step, peers)
+        return remote(
+            outgoing.at[peer], whole.at[column, me], rows_send.at[peer], rows_recv.at[me], dp=peer
+        )
+
+    def rows_arrival(step):
+        peer = lax.rem(me + peers - step, peers)
+        return remote(
+            outgoing.at[peer], whole.at[column, peer], rows_send.at[peer], rows_recv.at[peer], dp=peer
+        )
+
+    for step in range(1, peers):
+        rows_copy(step).start()
+    whole[column, me] = outgoing[me]
+
+    def part(shard, cut):
+        return weights.at[cut, pl.ds(pl.multiple_of(shard * depth, depth), depth)]
+
+    def weight_copy(where, source, cut, peer):
+        shard = source * 2 + core
+        return remote(
+            part(shard, cut), part(shard, cut), where.at[source, cut], w_recv.at[shard, cut], dp=peer
+        )
+
+    def weight_arrival(shard, cut):
+        return remote(
+            part(shard, cut), part(shard, cut), w_side.at[0, cut], w_recv.at[shard, cut], dp=twin
+        )
+
+    for cut in range(cuts):
+        for load in loads[5 + 2 * cut:7 + 2 * cut]:
+            load.wait()
+        pl.when(last)(lambda: weight_copy(w_up, chip, cut, above).start())
+        pl.when(inner)(lambda: weight_copy(w_down, chip, cut, below).start())
+        weight_copy(w_side, chip, cut, twin).start()
+
+    def relay(cut, step, onward):
+        @pl.when((chip >= step) & (last if onward else jnp.logical_not(last)))
+        def _():
+            source = chip - step
+            weight_arrival(source * 2 + core, cut).wait_recv()
+            if onward:
+                weight_copy(w_up, source, cut, above).start()
+            weight_copy(w_side, source, cut, twin).start()
+
+        @pl.when((chip + step < chips) & (inner if onward else jnp.logical_not(inner)))
+        def _():
+            source = chip + step
+            weight_arrival(source * 2 + core, cut).wait_recv()
+            if onward:
+                weight_copy(w_down, source, cut, below).start()
+            weight_copy(w_side, source, cut, twin).start()
+
+    def mp_copy(step, owned):
+        peer = lax.rem(column + step, groups)
+        return remote(
+            whole.at[column, owned], whole.at[column, owned], mp_send.at[peer, owned],
+            mp_recv.at[column, owned], mp=peer,
+        )
+
+    def mp_arrival(step, owned):
+        peer = lax.rem(column + step, groups)
+        return remote(
+            whole.at[peer, owned], whole.at[peer, owned], mp_send.at[peer, owned],
+            mp_recv.at[peer, owned], mp=peer,
+        )
+
+    for behind in range(peers):
+        if behind:
+            rows_arrival(behind).wait_recv()
+        for step in range(1, groups):
+            mp_copy(step, lax.rem(me + peers - behind, peers)).start()
+    for step in range(1, chips):
+        relay(0, step, True)
+    ahead = [(cut, step) for cut in range(1, cuts) for step in range(1, chips)]
+    for cut, step in ahead[:1]:
+        relay(cut, step, True)
+    for behind in range(peers):
+        for step in range(1, groups):
+            mp_arrival(step, lax.rem(me + peers - behind, peers)).wait_recv()
+    loads[3].wait()
+    loads[4].wait()
+    gain = gain_in[...].reshape(1, channels)
+
+    def block(group):
+        return whole[group].reshape(slots, width).astype(jnp.float32)
+
+    live = block(0)[:, :1] < 0.5 * filler
+    live_col = live.astype(jnp.float32)
+    total = jnp.zeros((slots, 1), jnp.float32)
+    for group in range(groups):
+        total += jnp.sum(block(group), axis=1, keepdims=True)
+    row_mean = jnp.where(live, total / channels, 0.0)
+    square = jnp.zeros((slots, 1), jnp.float32)
+    for group in range(groups):
+        centred = jnp.where(live, block(group) - row_mean, 0.0)
+        square += jnp.sum(centred * centred, axis=1, keepdims=True)
+    factor = lax.rsqrt(square / channels + epsilon)
+    for group in range(groups):
+        at = slice(group * width, (group + 1) * width)
+        centred = jnp.where(live, block(group) - row_mean, 0.0)
+        wide = centred * factor * gain[:, at] * live_col
+        normed[:, at] = wide.astype(jnp.bfloat16)
+        normed_t[at, :] = wide.T.astype(jnp.bfloat16)
+
+    def rows_of(shard):
+        return pl.ds(pl.multiple_of(shard * depth, depth), depth)
+
+    def t_copy(target):
+        return remote(
+            normed_t.at[rows_of(target * 2 + 1 - core)], sibling_t.at[target],
+            t_send.at[target], t_recv.at[target], dp=twin,
+        )
+
+    for target in range(chips):
+        t_copy(target).start()
+    def delta_copy(cut):
+        return remote(delta.at[cut], sibling_delta.at[cut], d_send.at[cut], d_recv.at[cut], dp=twin)
+
+    def project(cut):
+        for step in range(1, chips):
+            relay(cut, step, False)
+        for source in range(chips):
+            weight_arrival(source * 2 + 1 - core, cut).wait_recv()
+        act = jnp.dot(normed[...], weights[cut], preferred_element_type=jnp.float32)
+        at = slice(cut * 128, (cut + 1) * 128)
+        value_act = act[:, :128]
+        gate_sig = jax.nn.sigmoid(act[:, 128:])
+        upstream = upstream_in[:, at].astype(jnp.float32)
+        delta[cut, :, :128] = (upstream * gate_sig * live_col).astype(jnp.bfloat16)
+        delta[cut, :, 128:] = (
+            upstream * value_act * gate_sig * (1.0 - gate_sig) * live_col
+        ).astype(jnp.bfloat16)
+        delta_copy(cut).start()
+        gated_ref[:, at] = (value_act * gate_sig).astype(jnp.bfloat16)
+
+    def term(group):
+        rows = pl.ds(pl.multiple_of(group * width, width), width)
+        result = jnp.zeros((slots, width), jnp.float32)
+        for cut in range(cuts):
+            result += lax.dot_general(
+                delta[cut], weights[cut, rows, :], (((1,), (1,)), ((), ())),
+                preferred_element_type=jnp.float32,
+            )
+        return result.astype(jnp.bfloat16)
+
+    def x_copy(step):
+        peer = lax.rem(column + step, groups)
+        return remote(term_out.at[peer], term_in.at[column], x_send.at[peer], x_recv.at[column], mp=peer)
+
+    def x_arrival(step):
+        peer = lax.rem(column + step, groups)
+        return remote(term_out.at[peer], term_in.at[peer], x_send.at[peer], x_recv.at[peer], mp=peer)
+
+    def chip_sum(target, cut):
+        return jnp.dot(
+            normed_t[rows_of(target * 2 + core), :], delta[cut], preferred_element_type=jnp.float32
+        ) + jnp.dot(sibling_t[target], sibling_delta[cut], preferred_element_type=jnp.float32)
+
+    def hop(out, into, send, recv, target, cut, peer):
+        return remote(
+            out.at[cut, target], into.at[cut, target], send.at[cut, target], recv.at[cut, target],
+            dp=peer,
+        )
+
+    def up(target, cut, peer):
+        return hop(to_above, from_below, up_send, up_recv, target, cut, peer)
+
+    def down(target, cut, peer):
+        return hop(to_below, from_above, down_send, down_recv, target, cut, peer)
+
+    def send_sum(copy, out, into, target, cut, onward, behind, ahead):
+        own = chip_sum(target, cut)
+
+        @pl.when(onward)
+        def _():
+            copy(target, cut, behind).wait_recv()
+            out[cut, target] = (own + into[cut, target].astype(jnp.float32)).astype(jnp.bfloat16)
+
+        @pl.when(jnp.logical_not(onward))
+        def _():
+            out[cut, target] = own.astype(jnp.bfloat16)
+
+        copy(target, cut, ahead).start()
+
+    def chain(cut):
+        for step in range(chips - 1, 0, -1):
+            @pl.when(chip + step < chips)
+            def _():
+                send_sum(up, to_above, from_below, chip + step, cut, inner, below, above)
+
+            @pl.when(chip >= step)
+            def _():
+                send_sum(down, to_below, from_above, chip - step, cut, last, above, below)
+
+    project(0)
+    for cut, step in ahead[1:]:
+        relay(cut, step, True)
+    for target in range(chips):
+        t_copy(target).wait_recv()
+    for cut in range(cuts):
+        delta_copy(cut).wait_recv()
+        if cut == cuts - 1:
+            for step in range(1, groups):
+                peer = lax.rem(column + step, groups)
+                term_out[peer] = term(peer)
+                x_copy(step).start()
+        chain(cut)
+        if cut < cuts - 1:
+            project(cut + 1)
+
+    for cut in range(cuts):
+        at = slice(cut * 128, (cut + 1) * 128)
+        own = chip_sum(chip, cut)
+        value_grad_ref[:, at] = own[:, :128]
+        gate_grad_ref[:, at] = own[:, 128:]
+
+    input_grad = term(column).astype(jnp.float32)
+    for step in range(1, groups):
+        x_arrival(step).wait_recv()
+        input_grad += term_in[lax.rem(column + step, groups)].astype(jnp.float32)
+    input_grad_ref[...] = input_grad.astype(jnp.bfloat16)
+
+    def add(arrived, cut):
+        at = slice(cut * 128, (cut + 1) * 128)
+        value_grad_ref[:, at] += arrived[cut, chip, :, :128].astype(jnp.float32)
+        gate_grad_ref[:, at] += arrived[cut, chip, :, 128:].astype(jnp.float32)
+
+    for cut in range(cuts):
+        @pl.when(inner)
+        def _():
+            up(chip, cut, below).wait_recv()
+            add(from_below, cut)
+
+        @pl.when(last)
+        def _():
+            down(chip, cut, above).wait_recv()
+            add(from_above, cut)
+
+    value_grad_ref[...] *= scale
+    gate_grad_ref[...] *= scale
+
+    for step in range(1, peers):
+        rows_copy(step).wait_send()
+    for step in range(1, groups):
+        for owned in range(peers):
+            mp_copy(step, owned).wait_send()
+        x_copy(step).wait_send()
+    for source in range(chips):
+        t_copy(source).wait_send()
+    for cut in range(cuts):
+        delta_copy(cut).wait_send()
+        for source in range(chips):
+            weight_copy(w_side, source, cut, twin).wait_send()
+            pl.when(last & (source <= chip))(lambda: weight_copy(w_up, source, cut, above).wait_send())
+            pl.when(inner & (source >= chip))(lambda: weight_copy(w_down, source, cut, below).wait_send())
+            pl.when(source > chip)(lambda: up(source, cut, above).wait_send())
+            pl.when(source < chip)(lambda: down(source, cut, below).wait_send())
+
+
+def write_out(*refs):
+    count = len(refs) // 2
+    copies = [pltpu.make_async_copy(refs[i], refs[count + i], refs[-1].at[i]) for i in range(count)]
+    for copy in copies:
+        copy.start()
+    for copy in copies:
+        copy.wait()
+
+
+def body(frames, frame_owner, frame_valid, norm_gain, value_weight, gate_weight, grad_owned):
+    peers, groups = lax.axis_size("dp"), lax.axis_size("mp")
+    capacity = grad_owned.shape[2]
+    loaded, width = frames.shape
+    depth = value_weight.shape[0]
+    if peers % 2 or depth % 16 or capacity % 16 or loaded % 16 or width % 128 or groups * width != peers * depth:
+        return plain_body(
+            frames, frame_owner, frame_valid, norm_gain, value_weight, gate_weight, grad_owned
+        )
+    slots, chips, channels = peers * capacity, peers // 2, width * groups
+    cuts = width // 128
+    half, full = jnp.bfloat16, jnp.float32
+    dma = pltpu.SemaphoreType.DMA
+    hop = pltpu.VMEM((cuts, chips, depth, 256), half)
+    deltas = pltpu.VMEM((cuts, slots, 256), half)
+    vmem, hbm = pl.BlockSpec(memory_space=pltpu.VMEM), pl.BlockSpec(memory_space=pltpu.HBM)
+    outs = (
+        jax.ShapeDtypeStruct((slots, width), half),
+        jax.ShapeDtypeStruct((depth, width), full),
+        jax.ShapeDtypeStruct((depth, width), full),
+        jax.ShapeDtypeStruct((slots, width), half),
+    )
+    results = pl.pallas_call(
+        functools.partial(kernel, peers, groups, capacity, float(loaded * peers) ** (-0.5)),
+        out_shape=outs,
+        in_specs=[hbm] * 7,
+        out_specs=(vmem,) * 4,
+        scratch_shapes=[
+            pltpu.VMEM((loaded, width), half),
+            pltpu.VMEM((1, loaded), jnp.int32),
+            pltpu.VMEM((1, loaded), jnp.int32),
+            pltpu.VMEM((channels,), full),
+            pltpu.VMEM((slots, width), half),
+            pltpu.VMEM((peers, capacity, width), half),
+            pltpu.VMEM((groups, peers, capacity, width), half),
+            pltpu.VMEM((cuts, channels, 256), half),
+            pltpu.VMEM((slots, channels), half),
+            pltpu.VMEM((channels, slots), half),
+            pltpu.VMEM((chips, depth, slots), half),
+            deltas, deltas,
+            hop, hop, hop, hop,
+            pltpu.VMEM((groups, slots, width), half),
+            pltpu.VMEM((groups, slots, width), half),
+            dma((5 + 2 * cuts,)),
+            dma((peers,)), dma((peers,)), dma((groups, peers)), dma((groups, peers)),
+            dma((chips, cuts)), dma((chips, cuts)), dma((chips, cuts)), dma((peers, cuts)),
+            dma((chips,)), dma((chips,)), dma((cuts,)), dma((cuts,)),
+            dma((cuts, chips)), dma((cuts, chips)), dma((cuts, chips)), dma((cuts, chips)),
+            dma((groups,)), dma((groups,)),
+        ],
+        compiler_params=pltpu.CompilerParams(
+            collective_id=0, has_side_effects=True, vmem_limit_bytes=63 * 1024 * 1024
+        ),
+    )(
+        frames, frame_owner.reshape(1, loaded), frame_valid.reshape(1, loaded), norm_gain,
+        value_weight, gate_weight, grad_owned.reshape(slots, width),
+    )
+    gated, value_grad, gate_grad, input_grad = pl.pallas_call(
+        write_out,
+        out_shape=outs,
+        in_specs=[hbm] * 4,
+        out_specs=(hbm,) * 4,
+        scratch_shapes=[dma((4,))],
+    )(*results)
+    return (
+        gated.reshape(1, peers, capacity, width), value_grad, gate_grad,
+        input_grad.reshape(1, peers, capacity, width),
+    )
+
+
 def solution(mesh):
     placed = (
         P("dp", "mp"),

time: 160 us -> 88.4 us (0.55)
  waiting for transfers between devices: 102 us -> 0 us
  Pallas kernels: 0 us -> 87.5 us
  blocking collectives: 14.1 us -> 0 us
  between operations: 13.9 us -> 0.64 us
  starting transfers between devices: 9.88 us -> 0 us
  matrix products: 9.09 us -> 0 us
  other arithmetic: 6.05 us -> 0 us
  local copies, waits for them, and re-layouts: 4.37 us -> 0 us
    pallas_call x0 -> x2, Pallas kernels: none -> 87.5 us  [the longest x1 56.6 us: body(): pl.pallas_call(functools.partial(kernel, peers, groups, capacity, float(l...]
    reduce_scatter x1 -> x0, waiting for transfers between devices: 55.4 us -> none  [body(): lax.psum_scatter(column_term(normed_flat, both_delta), 'dp', scatter_dime...]
    unnamed x5 -> x0, waiting for transfers between devices: 23.7 us -> none
    all_to_all x2 -> x0, waiting for transfers between devices: 15.1 us -> none  [the longest x1 11.3 us: body(): lax.all_to_all(send_buffer, 'dp', split_axis=0, concat_axis=0, tiled=True)]
    all_gather x1 -> x0, blocking collectives: 14.1 us -> none  [body(): whole = lax.all_gather(received_rows, 'mp', axis=2, tiled=True)]
    all_to_all x2 -> x0, starting transfers between devices: 9.72 us -> none  [the longest x1 6.33 us: body(): lax.all_to_all(send_live, 'dp', split_axis=0, concat_axis=0, tiled=True)]
    dot_general x7 -> x0, matrix products: 9.09 us -> none  [the longest x1 2.96 us: column_term(): lax.dot_general(normed_flat, delta, (((0,), (0,)), ((), ())), preferred_e...]
    all_gather x2 -> x0, waiting for transfers between devices: 7.94 us -> none  [the longest x1 7.92 us: body(): lax.all_gather(value_weight, 'dp', axis=0, tiled=True)]
  transfers between devices with their start and end apart: 6 -> 0, of which waited for: 5 -> 0; matrix products, arithmetic and copies ran while one was open for 7% -> 0% of each run, Pallas kernels for 0% -> 0%
where the time goes in v2:
time: 88.4 us; the launch traced here: 88.2 us
  Pallas kernels  87.5 us (99%)
    pallas_call x1, Pallas kernels, body(): pl.pallas_call(functools.partial(kernel, peers, groups, capacity, float(l...  56.6 us
    pallas_call x1, Pallas kernels, body(): pl.pallas_call(write_out, out_shape=outs, in_specs=[hbm] * 4, out_specs=(...  30.9 us

profile of v2, /device:TPU:0, one launch (start us, length us, event | category | flops | bytes accessed | tf_op | source)
XLA Modules:
  0.0 88.2 jit_solution(8038744895391889283)
XLA Ops:
  0.6 56.6 %shard_map.102 = (bf16[256,384]{1,0:T(8,128)(2,1)}, f32[192,384]{1,0:T(8,128)}, f32[192,384]{1,0:T(8,128)}, bf16[256,384]{1,0:T(8,128)(2,1)}) custom-call(bf16[192,384]{1,0:T(8,128)(2,1)} %frames_ref.1, s32[1,192]{1,0:T(1,128)} %bitcast.6, s32[1,192]{1,0:T(1,128)} %bitcast.7, f32[1536]{0:T(1024)} %gain_ref.1, bf16[192,384]{1,0:T(8,128)(2,1)} %value_ref.1, ...), custom_call_target="tpu_custom_call" | custom-call | tf_op jit(solution)/shard_map/pallas_call | solution.py:484
  57.2 30.9 %shard_map.103 = (bf16[256,384]{1,0:T(8,128)(2,1)}, f32[192,384]{1,0:T(8,128)}, f32[192,384]{1,0:T(8,128)}, bf16[256,384]{1,0:T(8,128)(2,1)}) custom-call(bf16[256,384]{1,0:T(8,128)(2,1)} %get-tuple-element.12.refs_0_, f32[192,384]{1,0:T(8,128)} %get-tuple-element.13.refs_1_, f32[192,384]{1,0:T(8,128)} %get-tuple-element.14.refs_2_, ...), custom_call_target="tpu_custom_call" | custom-call | tf_op jit(solution)/shard_map/pallas_call | solution.py:519

commit v3 on v2

--- a/solution.py
+++ b/solution.py
@@ -219,11 +219,16 @@
             part(shard, cut), part(shard, cut), w_side.at[0, cut], w_recv.at[shard, cut], dp=twin
         )
 
+    def send_own(cut):
+        if cut < cuts:
+            pl.when(last)(lambda: weight_copy(w_up, chip, cut, above).start())
+            pl.when(inner)(lambda: weight_copy(w_down, chip, cut, below).start())
+
     for cut in range(cuts):
         for load in loads[5 + 2 * cut:7 + 2 * cut]:
             load.wait()
-        pl.when(last)(lambda: weight_copy(w_up, chip, cut, above).start())
-        pl.when(inner)(lambda: weight_copy(w_down, chip, cut, below).start())
+        if cut == 0:
+            send_own(cut)
         weight_copy(w_side, chip, cut, twin).start()
 
     def relay(cut, step, onward):
@@ -262,11 +267,18 @@
             rows_arrival(behind).wait_recv()
         for step in range(1, groups):
             mp_copy(step, lax.rem(me + peers - behind, peers)).start()
-    for step in range(1, chips):
-        relay(0, step, True)
-    ahead = [(cut, step) for cut in range(1, cuts) for step in range(1, chips)]
-    for cut, step in ahead[:1]:
-        relay(cut, step, True)
+    def relays(cut, steps):
+        if cut < cuts:
+            for step in steps:
+                relay(cut, step, True)
+                if step == 1:
+                    send_own(cut + 1)
+
+    relays(0, range(1, chips))
+    if chips < 2:
+        for cut in range(1, cuts):
+            send_own(cut)
+    relays(1, range(1, min(2, chips)))
     for behind in range(peers):
         for step in range(1, groups):
             mp_arrival(step, lax.rem(me + peers - behind, peers)).wait_recv()
@@ -377,6 +389,7 @@
 
     def chain(cut):
         for step in range(chips - 1, 0, -1):
+            relays(cut + 2, range(chips - step, chips - step + 1))
             @pl.when(chip + step < chips)
             def _():
                 send_sum(up, to_above, from_below, chip + step, cut, inner, below, above)
@@ -385,9 +398,8 @@
             def _():
                 send_sum(down, to_below, from_above, chip - step, cut, last, above, below)
 
+    relays(1, range(2, chips))
     project(0)
-    for cut, step in ahead[1:]:
-        relay(cut, step, True)
     for target in range(chips):
         t_copy(target).wait_recv()
     for cut in range(cuts):
@@ -451,12 +463,18 @@
 
 
 def write_out(*refs):
-    count = len(refs) // 2
-    copies = [pltpu.make_async_copy(refs[i], refs[count + i], refs[-1].at[i]) for i in range(count)]
-    for copy in copies:
-        copy.start()
-    for copy in copies:
-        copy.wait()
+    count = len(refs) // 3
+    for i, (source, result, held) in enumerate(
+        zip(refs[:count], refs[count:2 * count], refs[2 * count:3 * count])
+    ):
+        pltpu.make_async_copy(source, held, refs[-1].at[0, i]).start()
+    for i, (source, result, held) in enumerate(
+        zip(refs[:count], refs[count:2 * count], refs[2 * count:3 * count])
+    ):
+        pltpu.make_async_copy(source, held, refs[-1].at[0, i]).wait()
+        pltpu.make_async_copy(held, result, refs[-1].at[1, i]).start()
+    for i, (result, held) in enumerate(zip(refs[count:2 * count], refs[2 * count:3 * count])):
+        pltpu.make_async_copy(held, result, refs[-1].at[1, i]).wait()
 
 
 def body(frames, frame_owner, frame_valid, norm_gain, value_weight, gate_weight, grad_owned):
@@ -521,7 +539,7 @@
         out_shape=outs,
         in_specs=[hbm] * 4,
         out_specs=(hbm,) * 4,
-        scratch_shapes=[dma((4,))],
+        scratch_shapes=[pltpu.VMEM(out.shape, out.dtype) for out in outs] + [dma((2, 4))],
     )(*results)
     return (
         gated.reshape(1, peers, capacity, width), value_grad, gate_grad,

time: 88.4 us -> 57.4 us (0.65)
  Pallas kernels: 87.5 us -> 56.6 us
    pallas_call x1, Pallas kernels: 30.9 us -> 2.01 us  [body(): pl.pallas_call(write_out, out_shape=outs, in_specs=[hbm] * 4, out_specs=(...]
    pallas_call x1, Pallas kernels: 56.6 us -> 54.6 us  [body(): pl.pallas_call(functools.partial(kernel, peers, groups, capacity, float(l...]
where the time goes in v3:
time: 57.4 us; the launch traced here: 57.3 us
  Pallas kernels  56.6 us (99%)
  between operations  0.64 us (1%)
    pallas_call x1, Pallas kernels, body(): pl.pallas_call(functools.partial(kernel, peers, groups, capacity, float(l...  54.6 us
    pallas_call x1, Pallas kernels, body(): pl.pallas_call(write_out, out_shape=outs, in_specs=[hbm] * 4, out_specs=(...  2.01 us

profile of v3, /device:TPU:0, one launch (start us, length us, event | category | flops | bytes accessed | tf_op | source)
XLA Modules:
  0.0 57.3 jit_solution(15935731499533324079)
XLA Ops:
  0.6 54.6 %shard_map.102 = (bf16[256,384]{1,0:T(8,128)(2,1)}, f32[192,384]{1,0:T(8,128)}, f32[192,384]{1,0:T(8,128)}, bf16[256,384]{1,0:T(8,128)(2,1)}) custom-call(bf16[192,384]{1,0:T(8,128)(2,1)} %frames_ref.1, s32[1,192]{1,0:T(1,128)} %bitcast.6, s32[1,192]{1,0:T(1,128)} %bitcast.7, f32[1536]{0:T(1024)} %gain_ref.1, bf16[192,384]{1,0:T(8,128)(2,1)} %value_ref.1, ...), custom_call_target="tpu_custom_call" | custom-call | tf_op jit(solution)/shard_map/pallas_call | solution.py:502
  55.3 2.0 %shard_map.103 = (bf16[256,384]{1,0:T(8,128)(2,1)}, f32[192,384]{1,0:T(8,128)}, f32[192,384]{1,0:T(8,128)}, bf16[256,384]{1,0:T(8,128)(2,1)}) custom-call(bf16[256,384]{1,0:T(8,128)(2,1)} %get-tuple-element.12.refs_0_, f32[192,384]{1,0:T(8,128)} %get-tuple-element.13.refs_1_, f32[192,384]{1,0:T(8,128)} %get-tuple-element.14.refs_2_, ...), custom_call_target="tpu_custom_call" | custom-call | tf_op jit(solution)/shard_map/pallas_call | solution.py:537
